TPU v7x, 32 devices: a whole 2x2x4 slice. The times are simulated.
32 devices in a mesh: parts: 2 (over x), gx: 16 (over z, y, core).
Axes of the slice: x: 2, y: 2, z: 4, core: 2. Of those that a mesh axis runs over, the one named last changes fastest.
Arguments:
- positions: bfloat16 [3, 8, 32, 256, 128], P(None, None, 'gx', 'parts'), parts along dimension 3, may hold values from 0 to 1
- normals: bfloat16 [3, 8, 32, 256, 128], P(None, None, 'gx', 'parts'), parts along dimension 3, may hold values from -6 to 6
- counts: int32 [32, 256, 128], P('gx', 'parts'), parts along dimension 1, may hold values from 0 to 8
- screen: float32 [32, 256, 128], P('gx', 'parts'), parts along dimension 1, may hold values from 0.05 to 0.5
Outputs:
- solution_field: float32 [32, 256, 128], P('gx', 'parts'), parts along dimension 1
- residual: float32 [32, 256, 128], P('gx', 'parts'), parts along dimension 1
There are 2 independent parts, one for each index of `parts`. A program takes and returns all parts, laid end to end along the dimension named above; each array names one. Nothing has to cross between parts.
All inputs are finite; a program needn't handle non-finite values.
Results may differ from a plain program's by a relative error of at most 0.0003.
Values sent between devices are 32-bit elements; how exact they have to be, the bound alone decides.
A program may use at most 64 MiB of HBM per device.

v0:
```python
import jax
import jax.numpy as jnp
from jax import lax
from jax.sharding import PartitionSpec as P

ITERS = 3


def with_halo(shard, sides, width):
    for axis, dim in sides:
        peers, length = (lax.axis_size(axis), shard.shape[dim])
        up = [(i, (i + 1) % peers) for i in range(peers - 1)]
        down = [(j, i) for i, j in up]
        last = lax.slice_in_dim(shard, length - width, length, axis=dim)
        leading = lax.slice_in_dim(shard, 0, width, axis=dim)
        before = lax.ppermute(last, axis, up)
        after = lax.ppermute(leading, axis, down)
        shard = jnp.concatenate([before, shard, after], axis=dim)
    return shard


def spline_weights(fraction):
    return [0.5 * (1.0 - fraction) ** 2, 0.75 - (fraction - 0.5) ** 2, 0.5 * fraction * fraction]


def splat_cells(positions, normals, counts):
    slot_total = positions.shape[1]
    cells_x, cells_y, cells_z = counts.shape
    accums = [jnp.zeros((3, cells_x, cells_y, cells_z), jnp.float32) for offset_index in range(27)]
    for slot_index in range(slot_total):
        active = (counts > slot_index).astype(jnp.float32)
        vectors = normals[:, slot_index].astype(jnp.float32) * active
        fraction = positions[:, slot_index].astype(jnp.float32)
        along_x = spline_weights(fraction[0])
        along_y = spline_weights(fraction[1])
        along_z = spline_weights(fraction[2])
        for first_off in range(3):
            for second_off in range(3):
                planar = along_x[first_off] * along_y[second_off]
                for third_off in range(3):
                    place = first_off * 9 + second_off * 3 + third_off
                    accums[place] = accums[place] + vectors * (planar * along_z[third_off])
    padded = jnp.zeros((3, cells_x + 2, cells_y + 2, cells_z + 2), jnp.float32)
    for first_off in range(3):
        for second_off in range(3):
            for third_off in range(3):
                place = first_off * 9 + second_off * 3 + third_off
                padded = padded + jnp.pad(
                    accums[place],
                    (
                        (0, 0),
                        (first_off, 2 - first_off),
                        (second_off, 2 - second_off),
                        (third_off, 2 - third_off),
                    ),
                )
    return padded


def divergence(ghost_x, field):
    deriv_x = 0.5 * (ghost_x[2:] - ghost_x[:-2])
    padded_y = jnp.pad(field[1], ((0, 0), (1, 1), (0, 0)))
    deriv_y = 0.5 * (padded_y[:, 2:] - padded_y[:, :-2])
    padded_z = jnp.pad(field[2], ((0, 0), (0, 0), (1, 1)))
    deriv_z = 0.5 * (padded_z[:, :, 2:] - padded_z[:, :, :-2])
    return deriv_x + deriv_y + deriv_z


def operate(field, screen):
    cells_x, cells_y, cells_z = field.shape
    extended = with_halo(field, (("gx", 0),), 1)
    padded = jnp.pad(extended, ((0, 0), (1, 1), (1, 1)))
    table = {1: 1.0, 2: 0.5, 3: 0.25}
    total = jnp.zeros_like(field)
    for offset_x in range(3):
        for offset_y in range(3):
            for offset_z in range(3):
                moved = abs(offset_x - 1) + abs(offset_y - 1) + abs(offset_z - 1)
                if moved > 0:
                    total = (
                        total
                        + table[moved]
                        * padded[
                            offset_x : offset_x + cells_x,
                            offset_y : offset_y + cells_y,
                            offset_z : offset_z + cells_z,
                        ]
                    )
    return screen * field + 0.25 * (14.0 * field - total)


def squares(residual):
    return lax.psum(jnp.sum(residual * residual), "gx")


def local(positions, normals, counts, screen):
    padded = splat_cells(positions, normals, counts)
    interior = padded[:, 1:-1, 1:-1, 1:-1]
    low_rim = padded[:, 0, 1:-1, 1:-1]
    high_rim = padded[:, -1, 1:-1, 1:-1]
    rims = jnp.stack([low_rim, high_rim], axis=1)
    arrived = with_halo(rims, (("gx", 1),), 1)
    field = interior.at[:, 0].add(arrived[:, 0]).at[:, -1].add(arrived[:, 3])
    ghost_x = with_halo(field[0], (("gx", 0),), 1)
    right_side = divergence(ghost_x, field)
    solution_field = jnp.zeros_like(right_side)
    residual = right_side
    direction = right_side
    norm_now = squares(residual)
    for step_index in range(ITERS):
        image = operate(direction, screen)
        alpha = norm_now / lax.psum(jnp.sum(direction * image), "gx")
        solution_field = solution_field + alpha * direction
        residual = residual - alpha * image
        norm_next = squares(residual)
        direction = residual + norm_next / norm_now * direction
        norm_now = norm_next
    return (solution_field, residual)


def solution(mesh):
    placed = (
        P(None, None, "gx", "parts", None),
        P(None, None, "gx", "parts", None),
        P("gx", "parts", None),
        P("gx", "parts", None),
    )
    return jax.shard_map(
        local,
        mesh=mesh,
        in_specs=placed,
        out_specs=(P("gx", "parts", None), P("gx", "parts", None)),
        check_vma=False,
    )
```

profile of v0, /device:TPU:0, one launch (start us, length us, event | category | flops | bytes accessed | tf_op | source)
XLA Modules:
  0.0 233.3 jit_solution(10899553517678850583)
XLA Ops:
  0.6 1.8 slice_convert_fusion.7
  8.1 0.5 copy-done.2
  8.7 0.6 copy-done
  9.7 0.4 fusion.55
  10.1 0.4 fusion.54
  10.5 0.4 fusion.53
  11.8 0.4 fusion.50
  12.3 0.4 fusion.49
  13.6 0.4 fusion.46
  14.0 0.4 fusion.45
  14.5 0.4 fusion.44
  14.9 0.6 fusion.43
  15.5 0.4 fusion.42
  16.0 0.4 fusion.41
  17.3 0.4 fusion.38
  17.7 0.4 fusion.37
  18.1 0.4 fusion.36
  19.4 0.4 fusion.33
  19.9 0.4 fusion.32
  20.3 0.4 fusion.31
  21.2 5.2 %pad_add_fusion = f32[3,4,130,130]{3,2,1,0:T(8,128)S(1)} fusion(f32[3,2,128,128]{3,2,1,0:T(8,128)S(1)} %fusion.56, f32[3,2,128,128]{3,2,1,0:T(8,128)S(1)} %fusion.55, f32[3,2,128,128]{3,2,1,0:T(8,128)S(1)} %fusion.54, f32[3,2,128,128]{3,2,1,0:T(8,128)S(1)} %fusion.53, f32[3,2,128,128]{3,2,1,0:T(8,128)S(1)} %fusion.52, f32[3,2,128,128]{3,2,1,0:T(8,128)S(1)} %fusion.51, ...), kind=kLoop, calls=%fused_computation | loop fusion | flops 5272800 | bytes 11428032 | tf_op jit(solution)/shard_map/add | solution.py:48
  26.6 2.4 %collective-permute-start = (f32[3,1,128,128]{3,2,1,0:T(8,128)S(1)}, f32[3,1,128,128]{3,2,1,0:T(8,128)S(1)}, u32[]{:S(2)}, u32[]{:S(2)}) collective-permute-start(f32[3,1,128,128]{3,2,1,0:T(8,128)S(1)} %get-tuple-element.42), channel_id=1, source_target_pairs={{0,1},{1,2},{2,3},{3,4},{4,5},{5,6},{6,7},{7,8},{8,9},{9,10},{10,1... | collective-permute-start | bytes 589832 | tf_op jit(solution)/shard_map/ppermute | solution.py:16
  28.9 1.3 collective-permute-start.1
  30.6 3.8 %collective-permute-done.1 = f32[3,1,128,128]{3,2,1,0:T(8,128)S(1)} collective-permute-done((f32[3,1,128,128]{3,2,1,0:T(8,128)S(1)}, f32[3,1,128,128]{3,2,1,0:T(8,128)S(1)}, u32[]{:S(2)}, u32[]{:S(2)}) %collective-permute-start.1) | collective-permute-done | bytes 196640 | tf_op jit(solution)/shard_map/ppermute | solution.py:17
  34.5 6.1 %collective-permute-start.3 = (f32[1,128,128]{2,1,0:T(8,128)S(1)}, f32[1,128,128]{2,1,0:T(8,128)S(1)}, u32[]{:S(2)}, u32[]{:S(2)}) collective-permute-start(f32[1,128,128]{2,1,0:T(8,128)S(1)} %slice_bitcast_fusion.27), channel_id=1, source_target_pairs={{0,1},{1,2},{2,3},{3,4},{4,5},{5,6},{6,7},{7,8},{8,9},{9,10},{10,1... | collective-permute-start | bytes 196616 | tf_op jit(solution)/shard_map/ppermute | solution.py:16
  40.6 1.3 collective-permute-start.2
  41.9 1.8 collective-permute-done.2
  43.9 1.3 collective-permute-start.5
  45.2 5.8 %collective-permute-start.4 = (f32[1,128,128]{2,1,0:T(8,128)S(1)}, f32[1,128,128]{2,1,0:T(8,128)S(1)}, u32[]{:S(2)}, u32[]{:S(2)}) collective-permute-start(f32[1,128,128]{2,1,0:T(8,128)S(1)} %get-tuple-element.274), channel_id=1, source_target_pairs={{0,1},{1,2},{2,3},{3,4},{4,5},{5,6},{6,7},{7,8},{8,9},{9,10},{10,1... | collective-permute-start | bytes 196616 | tf_op jit(solution)/shard_map/ppermute | solution.py:16
  51.0 0.9 collective-permute-done.4
  52.1 1.2 multiply_reduce_fusion.4
  53.3 33.9 %all-reduce.32 = (f32[]{:T(128)}, f32[]{:T(128)}) all-reduce(f32[]{:T(128)} %get-tuple-element.27, f32[]{:T(128)} %get-tuple-element.26), channel_id=1, replica_groups=mesh['parts'=2,'gx'=16] {'gx'}, use_global_device_ids=true, to_apply=%region_1.2 | all-reduce | flops 2 | bytes 16 | tf_op jit(solution)/shard_map/psum | solution.py:93
  88.5 0.6 multiply_reduce_fusion.3
  89.2 30.1 %psum.44 = f32[]{:T(128)} all-reduce(f32[]{:T(128)} %multiply_reduce_fusion.3), channel_id=1, replica_groups=mesh['parts'=2,'gx'=16] {'gx'}, use_global_device_ids=true, to_apply=%region_5.6 | all-reduce | flops 1 | bytes 8 | tf_op jit(solution)/shard_map/psum | solution.py:93
  120.7 1.3 collective-permute-start.7
  122.0 3.0 %collective-permute-start.6 = (f32[1,128,128]{2,1,0:T(8,128)S(1)}, f32[1,128,128]{2,1,0:T(8,128)S(1)}, u32[]{:S(2)}, u32[]{:S(2)}) collective-permute-start(f32[1,128,128]{2,1,0:T(8,128)S(1)} %get-tuple-element.272), channel_id=1, source_target_pairs={{0,1},{1,2},{2,3},{3,4},{4,5},{5,6},{6,7},{7,8},{8,9},{9,10},{10,1... | collective-permute-start | bytes 196616 | tf_op jit(solution)/shard_map/ppermute | solution.py:16
  125.0 0.9 collective-permute-done.6
  126.1 1.2 multiply_reduce_fusion.2
  127.3 31.6 %psum.45 = f32[]{:T(128)} all-reduce(f32[]{:T(128)} %get-tuple-element.34), channel_id=1, replica_groups=mesh['parts'=2,'gx'=16] {'gx'}, use_global_device_ids=true, to_apply=%region_7.8 | all-reduce | flops 1 | bytes 8 | tf_op jit(solution)/shard_map/psum | solution.py:112
  160.3 0.6 multiply_reduce_fusion.1
  160.9 30.1 %psum.46 = f32[]{:T(128)} all-reduce(f32[]{:T(128)} %get-tuple-element.32), channel_id=1, replica_groups=mesh['parts'=2,'gx'=16] {'gx'}, use_global_device_ids=true, to_apply=%region_9.10 | all-reduce | flops 1 | bytes 8 | tf_op jit(solution)/shard_map/psum | solution.py:93
  192.4 1.3 collective-permute-start.9
  193.7 3.0 %collective-permute-start.8 = (f32[1,128,128]{2,1,0:T(8,128)S(1)}, f32[1,128,128]{2,1,0:T(8,128)S(1)}, u32[]{:S(2)}, u32[]{:S(2)}) collective-permute-start(f32[1,128,128]{2,1,0:T(8,128)S(1)} %get-tuple-element.270), channel_id=1, source_target_pairs={{0,1},{1,2},{2,3},{3,4},{4,5},{5,6},{6,7},{7,8},{8,9},{9,10},{10,1... | collective-permute-start | bytes 196616 | tf_op jit(solution)/shard_map/ppermute | solution.py:16
  196.7 0.9 collective-permute-done.8
  197.8 1.2 multiply_reduce_fusion
  199.0 31.6 %psum.47 = f32[]{:T(128)} all-reduce(f32[]{:T(128)} %get-tuple-element.30), channel_id=1, replica_groups=mesh['parts'=2,'gx'=16] {'gx'}, use_global_device_ids=true, to_apply=%region_11.12 | all-reduce | flops 1 | bytes 8 | tf_op jit(solution)/shard_map/psum | solution.py:112
  232.0 0.7 multiply_add_fusion
  232.7 0.7 multiply_subtract_fusion
  (72 shorter events, 11.2 us)
Async XLA Ops:
  7.7 0.9 copy-start.2
  7.8 1.4 copy-start
  26.6 3.9 %collective-permute-start = (f32[3,1,128,128]{3,2,1,0:T(8,128)S(1)}, f32[3,1,128,128]{3,2,1,0:T(8,128)S(1)}, u32[]{:S(2)}, u32[]{:S(2)}) collective-permute-start(f32[3,1,128,128]{3,2,1,0:T(8,128)S(1)} %get-tuple-element.42), channel_id=1, source_target_pairs={{0,1},{1,2},{2,3},{3,4},{4,5},{5,6},{6,7},{7,8},{8,9},{9,10},{10,1... | collective-permute-start | bytes 589832 | tf_op jit(solution)/shard_map/ppermute | solution.py:16
  28.9 5.5 %collective-permute-start.1 = (f32[3,1,128,128]{3,2,1,0:T(8,128)S(1)}, f32[3,1,128,128]{3,2,1,0:T(8,128)S(1)}, u32[]{:S(2)}, u32[]{:S(2)}) collective-permute-start(f32[3,1,128,128]{3,2,1,0:T(8,128)S(1)} %get-tuple-element.41), channel_id=1, source_target_pairs={{1,0},{2,1},{3,2},{4,3},{5,4},{6,5},{7,6},{8,7},{9,8},{10,9},{11,1... | collective-permute-start | bytes 589832 | tf_op jit(solution)/shard_map/ppermute | solution.py:17
  30.6 21.5 %copy-start.1 = (f32[2,128,128]{2,1,0:T(8,128)S(1)}, f32[2,128,128]{2,1,0:T(8,128)}, u32[]{:S(2)}) copy-start(f32[2,128,128]{2,1,0:T(8,128)} %param.11) | copy-start | bytes 393220
  34.5 7.4 %collective-permute-start.3 = (f32[1,128,128]{2,1,0:T(8,128)S(1)}, f32[1,128,128]{2,1,0:T(8,128)S(1)}, u32[]{:S(2)}, u32[]{:S(2)}) collective-permute-start(f32[1,128,128]{2,1,0:T(8,128)S(1)} %slice_bitcast_fusion.27), channel_id=1, source_target_pairs={{0,1},{1,2},{2,3},{3,4},{4,5},{5,6},{6,7},{7,8},{8,9},{9,10},{10,1... | collective-permute-start | bytes 196616 | tf_op jit(solution)/shard_map/ppermute | solution.py:16
  40.6 3.1 %collective-permute-start.2 = (f32[1,128,128]{2,1,0:T(8,128)S(1)}, f32[1,128,128]{2,1,0:T(8,128)S(1)}, u32[]{:S(2)}, u32[]{:S(2)}) collective-permute-start(f32[1,128,128]{2,1,0:T(8,128)S(1)} %slice_bitcast_fusion.28), channel_id=1, source_target_pairs={{1,0},{2,1},{3,2},{4,3},{5,4},{6,5},{7,6},{8,7},{9,8},{10,9},{11,1... | collective-permute-start | bytes 196616 | tf_op jit(solution)/shard_map/ppermute | solution.py:17
  43.9 7.1 %collective-permute-start.5 = (f32[1,128,128]{2,1,0:T(8,128)S(1)}, f32[1,128,128]{2,1,0:T(8,128)S(1)}, u32[]{:S(2)}, u32[]{:S(2)}) collective-permute-start(f32[1,128,128]{2,1,0:T(8,128)S(1)} %get-tuple-element.275), channel_id=1, source_target_pairs={{1,0},{2,1},{3,2},{4,3},{5,4},{6,5},{7,6},{8,7},{9,8},{10,9},{11,1... | collective-permute-start | bytes 196616 | tf_op jit(solution)/shard_map/ppermute | solution.py:17
  45.2 6.7 %collective-permute-start.4 = (f32[1,128,128]{2,1,0:T(8,128)S(1)}, f32[1,128,128]{2,1,0:T(8,128)S(1)}, u32[]{:S(2)}, u32[]{:S(2)}) collective-permute-start(f32[1,128,128]{2,1,0:T(8,128)S(1)} %get-tuple-element.274), channel_id=1, source_target_pairs={{0,1},{1,2},{2,3},{3,4},{4,5},{5,6},{6,7},{7,8},{8,9},{9,10},{10,1... | collective-permute-start | bytes 196616 | tf_op jit(solution)/shard_map/ppermute | solution.py:16
  120.7 4.3 %collective-permute-start.7 = (f32[1,128,128]{2,1,0:T(8,128)S(1)}, f32[1,128,128]{2,1,0:T(8,128)S(1)}, u32[]{:S(2)}, u32[]{:S(2)}) collective-permute-start(f32[1,128,128]{2,1,0:T(8,128)S(1)} %get-tuple-element.273), channel_id=1, source_target_pairs={{1,0},{2,1},{3,2},{4,3},{5,4},{6,5},{7,6},{8,7},{9,8},{10,9},{11,1... | collective-permute-start | bytes 196616 | tf_op jit(solution)/shard_map/ppermute | solution.py:17
  122.0 3.9 %collective-permute-start.6 = (f32[1,128,128]{2,1,0:T(8,128)S(1)}, f32[1,128,128]{2,1,0:T(8,128)S(1)}, u32[]{:S(2)}, u32[]{:S(2)}) collective-permute-start(f32[1,128,128]{2,1,0:T(8,128)S(1)} %get-tuple-element.272), channel_id=1, source_target_pairs={{0,1},{1,2},{2,3},{3,4},{4,5},{5,6},{6,7},{7,8},{8,9},{9,10},{10,1... | collective-permute-start | bytes 196616 | tf_op jit(solution)/shard_map/ppermute | solution.py:16
  192.4 4.3 %collective-permute-start.9 = (f32[1,128,128]{2,1,0:T(8,128)S(1)}, f32[1,128,128]{2,1,0:T(8,128)S(1)}, u32[]{:S(2)}, u32[]{:S(2)}) collective-permute-start(f32[1,128,128]{2,1,0:T(8,128)S(1)} %get-tuple-element.271), channel_id=1, source_target_pairs={{1,0},{2,1},{3,2},{4,3},{5,4},{6,5},{7,6},{8,7},{9,8},{10,9},{11,1... | collective-permute-start | bytes 196616 | tf_op jit(solution)/shard_map/ppermute | solution.py:17
  193.7 3.9 %collective-permute-start.8 = (f32[1,128,128]{2,1,0:T(8,128)S(1)}, f32[1,128,128]{2,1,0:T(8,128)S(1)}, u32[]{:S(2)}, u32[]{:S(2)}) collective-permute-start(f32[1,128,128]{2,1,0:T(8,128)S(1)} %get-tuple-element.270), channel_id=1, source_target_pairs={{0,1},{1,2},{2,3},{3,4},{4,5},{5,6},{6,7},{7,8},{8,9},{9,10},{10,1... | collective-permute-start | bytes 196616 | tf_op jit(solution)/shard_map/ppermute | solution.py:16
where the time goes:
time: 234 us; the launch traced here: 233 us
  blocking collectives  157 us (67%)
  other arithmetic  31.6 us (14%)
  starting transfers between devices  26.7 us (11%)
  waiting for transfers between devices  8.26 us (4%)
  between operations  7.92 us (3%)
    psum x3, blocking collectives, squares(): return lax.psum(jnp.sum(residual * residual), 'gx')  94.1 us
    psum x2, blocking collectives, local(): alpha = norm_now / lax.psum(jnp.sum(direction * image), 'gx')  63.2 us
    ppermute x5, starting transfers between devices, with_halo(): before = lax.ppermute(last, axis, up)  20.3 us
    add x27, other arithmetic, splat_cells(): accums[place] = accums[place] + vectors * (planar * along_z[third_off])  11.9 us
    ppermute x5, starting transfers between devices, with_halo(): after = lax.ppermute(leading, axis, down)  6.46 us
    ppermute x5, waiting for transfers between devices, with_halo(): after = lax.ppermute(leading, axis, down)  5.65 us
    mul x36, other arithmetic, splat_cells(): accums[place] = accums[place] + vectors * (planar * along_z[third_off])  5.35 us
    add x1, other arithmetic, splat_cells(): padded + jnp.pad(accums[place], ((0, 0), (first_off, 2 - first_off), (sec...  5.2 us
  transfers between devices with their start and end apart: 10, of which 5 were waited for; matrix products, arithmetic and copies ran while one was open for 0% of the time, Pallas kernels for 0%

commit v1 on v0

v1 whole, which is shorter than its diff:
```python
import functools

import jax
import jax.numpy as jnp
from jax import lax
from jax.experimental import pallas as pl
from jax.experimental.pallas import tpu as pltpu
from jax.sharding import PartitionSpec as P

ITERS = 3
SHIFT = 2.25
CHUNK = 32
MESH = pl.DeviceIdType.MESH


def lane_before(a):
    lane = lax.broadcasted_iota(jnp.int32, a.shape, 1)
    return jnp.where(lane == 0, 0.0, pltpu.roll(a, 1, 1))


def lane_after(a):
    lane = lax.broadcasted_iota(jnp.int32, a.shape, 1)
    size = a.shape[1]
    return jnp.where(lane == size - 1, 0.0, pltpu.roll(a, size - 1, 1))


def row_before(a):
    row = lax.broadcasted_iota(jnp.int32, a.shape, 0)
    return jnp.where(row == 0, 0.0, pltpu.roll(a, 1, 0))


def row_after(a):
    row = lax.broadcasted_iota(jnp.int32, a.shape, 0)
    size = a.shape[0]
    return jnp.where(row == size - 1, 0.0, pltpu.roll(a, size - 1, 0))


def taps(m0, m1, m2):
    twice = m1 + m1
    return (m0 - twice) + m2, (m0 + twice) - (m2 + m2), m2


def gather_moments(pos, nrm, cnt, c, rows, half, plane, slots):
    part = slice(8 * half, 8 * half + 8)
    live = cnt[plane, rows, :][part]
    sums = [None] * 27
    for s in range(slots):
        n = nrm[c, s, plane, rows, :].astype(jnp.float32)[part]
        x = pos[0, s, plane, rows, :].astype(jnp.float32)[part]
        y = pos[1, s, plane, rows, :].astype(jnp.float32)[part]
        z = pos[2, s, plane, rows, :].astype(jnp.float32)[part]
        tx = jnp.where(live > s, n, 0.0)
        for p in range(3):
            if p:
                tx = tx * x
            ty = tx
            for q in range(3):
                if q:
                    ty = ty * y
                tz = ty
                for r in range(3):
                    if r:
                        tz = tz * z
                    at = 9 * p + 3 * q + r
                    sums[at] = tz if sums[at] is None else sums[at] + tz
    return sums


def kernel(n, slots, pos_hbm, nrm_hbm, cnt_hbm, scr_hbm, sol_ref, res_ref,
           pos, nrm, cnt, scr, g, out_l, out_r, in_l, in_r, v, halo, part, parts,
           load_sem, send_sem, recv_sem, psend, precv):
    me = lax.axis_index("gx")
    my_part = lax.axis_index("parts")
    ny = cnt.shape[1]
    chunks = ny // CHUNK
    has_left, has_right = me > 0, me < n - 1

    def peer(i):
        return {"parts": my_part, "gx": i}

    def loads(k):
        rows = pl.ds(pl.multiple_of(k * CHUNK, CHUNK), CHUNK)
        return (
            pltpu.make_async_copy(pos_hbm.at[:, :, :, rows, :], pos.at[:, :, :, rows, :], load_sem.at[0, k]),
            pltpu.make_async_copy(nrm_hbm.at[:, :, :, rows, :], nrm.at[:, :, :, rows, :], load_sem.at[1, k]),
            pltpu.make_async_copy(cnt_hbm.at[:, rows, :], cnt.at[:, rows, :], load_sem.at[2, k]),
        )

    for k in range(chunks):
        for copy in loads(k):
            copy.start()
    scr_copy = pltpu.make_async_copy(scr_hbm, scr, load_sem.at[3, 0])
    scr_copy.start()

    barrier = pltpu.get_barrier_semaphore()

    @pl.loop(1, n)
    def _(d):
        pl.semaphore_signal(barrier, inc=1, device_id=peer(lax.rem(me + d, n)), device_id_type=MESH)

    @pl.loop(0, chunks)
    def _(k):
        for copy in loads(k):
            copy.wait()

        @pl.loop(0, CHUNK // 16)
        def _(j):
            start = pl.multiple_of(k * CHUNK + j * 16, 16)
            rows = pl.ds(start, 16)

            @pl.loop(0, 3)
            def _(c):
                for half in range(2):
                    low = gather_moments(pos, nrm, cnt, c, rows, half, 0, slots)
                    high = gather_moments(pos, nrm, cnt, c, rows, half, 1, slots)
                    own = pl.ds(pl.multiple_of(start + 8 * half, 8), 8)
                    for q in range(3):
                        planes = [[], [], [], []]
                        for r in range(3):
                            at = 3 * q + r
                            a = taps(low[at], low[9 + at], low[18 + at])
                            b = taps(high[at], high[9 + at], high[18 + at])
                            planes[0].append(a[0])
                            planes[1].append(a[1] + b[0])
                            planes[2].append(a[2] + b[1])
                            planes[3].append(b[2])
                        for i in range(4):
                            t = taps(*planes[i])
                            g[c, i, q, own, :] = lane_after(t[0]) + t[1] + lane_before(t[2])

    def along_y(c, i):
        t = taps(g[c, i, 0], g[c, i, 1], g[c, i, 2])
        return row_after(t[0]) + t[1] + row_before(t[2])

    def across(i):
        fy = along_y(1, i)
        fz = along_y(2, i)
        return (row_after(fy) - row_before(fy)) + (lane_after(fz) - lane_before(fz))

    scale = 1.0 / 16.0
    for i in range(4):
        v[i // 2, i % 2] = along_y(0, i)
    out_l[0] = scale * v[0, 0]
    out_l[1] = scale * (v[0, 1] + across(0))
    out_r[0] = scale * (across(3) - v[1, 0])
    out_r[1] = -scale * v[1, 1]

    pl.semaphore_wait(barrier, n - 1)

    def to_left(src, dst, at):
        return pltpu.make_async_remote_copy(
            src_ref=src, dst_ref=dst, send_sem=send_sem.at[0, at], recv_sem=recv_sem.at[0, at],
            device_id=peer(jnp.maximum(me - 1, 0)), device_id_type=MESH)

    def to_right(src, dst, at):
        return pltpu.make_async_remote_copy(
            src_ref=src, dst_ref=dst, send_sem=send_sem.at[1, at], recv_sem=recv_sem.at[1, at],
            device_id=peer(jnp.minimum(me + 1, n - 1)), device_id_type=MESH)

    pairs = [(to_left(out_l, in_r, 0), to_right(out_r, in_l, 0))]
    for k in range(3):
        pairs.append((to_left(v.at[k, 0], halo.at[k, 1], k + 1),
                      to_right(v.at[k, 1], halo.at[k, 0], k + 1)))

    def begin(at):
        @pl.when(has_left)
        def _():
            pairs[at][0].start()

        @pl.when(has_right)
        def _():
            pairs[at][1].start()

    def arrive(at):
        @pl.when(has_right)
        def _():
            pairs[at][0].wait_recv()

        @pl.when(has_left)
        def _():
            pairs[at][1].wait_recv()

    begin(0)
    inner0 = across(1) + v[1, 0] - jnp.where(has_left, v[0, 0], 0.0)
    inner1 = across(2) + jnp.where(has_right, v[1, 1], 0.0) - v[0, 1]
    v[0, 0] = scale * inner0
    v[0, 1] = scale * inner1
    @pl.when(jnp.logical_not(has_left))
    def _():
        in_l[...] = jnp.zeros_like(in_l)
        for k in range(3):
            halo[k, 0] = jnp.zeros_like(halo[k, 0])

    @pl.when(jnp.logical_not(has_right))
    def _():
        in_r[...] = jnp.zeros_like(in_r)
        for k in range(3):
            halo[k, 1] = jnp.zeros_like(halo[k, 1])

    scr_copy.wait()
    arrive(0)
    v[0, 0] = v[0, 0] + (in_l[0] + in_r[0])
    v[0, 1] = v[0, 1] + (in_l[1] + in_r[1])

    def smooth(a, b, c):
        u = a + (b + b) + c
        u = row_before(u) + (u + u) + row_after(u)
        return lane_before(u) + (u + u) + lane_after(u)

    def fold(a):
        return jnp.sum(a, axis=0, keepdims=True)

    def dot(i, j):
        return fold(v[i, 0] * v[j, 0] + v[i, 1] * v[j, 1])

    for k in range(3):
        begin(k + 1)
        part[2 * k:2 * k + 1, :] = dot(k, k)
        if k:
            part[2 * k - 1:2 * k, :] = dot(k - 1, k)
        arrive(k + 1)
        a, b = v[k, 0], v[k, 1]
        v[k + 1, 0] = (scr[0] + (4.0 - SHIFT)) * a - scale * smooth(halo[k, 0], a, b)
        v[k + 1, 1] = (scr[1] + (4.0 - SHIFT)) * b - scale * smooth(a, b, halo[k, 1])
    part[5:6, :] = dot(2, 3)
    part[6:8, :] = jnp.zeros((2, part.shape[1]), jnp.float32)

    def spread(d):
        return pltpu.make_async_remote_copy(
            src_ref=part, dst_ref=parts.at[d], send_sem=psend.at[d], recv_sem=precv.at[d],
            device_id=peer(lax.rem(me + d, n)), device_id_type=MESH)

    @pl.loop(1, n)
    def _(d):
        spread(d).start()

    @pl.loop(1, n)
    def _(d):
        spread(d).wait_recv()

    def order(d, total):
        return total + parts[d]

    parts[0] = part[...]
    total = lax.fori_loop(0, n, order, jnp.zeros(part.shape, jnp.float32))
    total = jnp.sum(total, axis=1, keepdims=True)
    moment = [jnp.broadcast_to(total[k:k + 1, :], (8, 128)) for k in range(6)]

    def inner(a, b):
        terms = {}
        for i, s in enumerate(a):
            for j, t in enumerate(b):
                terms[i + j] = s * t if i + j not in terms else terms[i + j] + s * t
        out = None
        for k, s in terms.items():
            out = s * moment[k] if out is None else out + s * moment[k]
        return out

    one = jnp.ones((8, 128), jnp.float32)
    none = jnp.zeros((8, 128), jnp.float32)
    sol, res, way, rr = [], [one], [one], moment[0]
    for step in range(ITERS):
        image = [SHIFT * s for s in way] + [none]
        image = [image[k] + (way[k - 1] if k else none) for k in range(len(image))]
        alpha = rr / inner(way, image)
        sol = [(sol[k] if k < len(sol) else none) + alpha * s for k, s in enumerate(way)]
        res = [(res[k] if k < len(res) else none) - alpha * s for k, s in enumerate(image)]
        if step < ITERS - 1:
            new = inner(res, res)
            beta = new / rr
            way = [s + (beta * way[k] if k < len(way) else none) for k, s in enumerate(res)]
            rr = new

    sol = [s[0:1, :] for s in sol]
    res = [s[0:1, :] for s in res]
    for i in range(2):
        sol_ref[i] = sol[0] * v[0, i] + sol[1] * v[1, i] + sol[2] * v[2, i]
        res_ref[i] = res[0] * v[0, i] + res[1] * v[1, i] + res[2] * v[2, i] + res[3] * v[3, i]

    @pl.loop(1, n)
    def _(d):
        spread(d).wait_send()

    @pl.when(has_left)
    def _():
        for pair in pairs:
            pair[0].wait_send()

    @pl.when(has_right)
    def _():
        for pair in pairs:
            pair[1].wait_send()


def local(n, positions, normals, counts, screen):
    slots = positions.shape[1]
    plane = counts.shape[1:]
    chunks = plane[0] // CHUNK
    f32 = jnp.float32
    out = jax.ShapeDtypeStruct(counts.shape, f32)
    return tuple(pl.pallas_call(
        functools.partial(kernel, n, slots),
        out_shape=(out, out),
        in_specs=[pl.BlockSpec(memory_space=pl.ANY)] * 4,
        out_specs=(pl.BlockSpec(memory_space=pltpu.VMEM),) * 2,
        scratch_shapes=[
            pltpu.VMEM(positions.shape, positions.dtype),
            pltpu.VMEM(normals.shape, normals.dtype),
            pltpu.VMEM(counts.shape, counts.dtype),
            pltpu.VMEM(screen.shape, f32),
            pltpu.VMEM((3, 4, 3) + plane, f32),
            pltpu.VMEM((2,) + plane, f32),
            pltpu.VMEM((2,) + plane, f32),
            pltpu.VMEM((2,) + plane, f32),
            pltpu.VMEM((2,) + plane, f32),
            pltpu.VMEM((4, 2) + plane, f32),
            pltpu.VMEM((3, 2) + plane, f32),
            pltpu.VMEM((8, 128), f32),
            pltpu.VMEM((n, 8, 128), f32),
            pltpu.SemaphoreType.DMA((4, chunks)),
            pltpu.SemaphoreType.DMA((2, 4)),
            pltpu.SemaphoreType.DMA((2, 4)),
            pltpu.SemaphoreType.DMA((n,)),
            pltpu.SemaphoreType.DMA((n,)),
        ],
        compiler_params=pltpu.CompilerParams(
            collective_id=0, has_side_effects=True, vmem_limit_bytes=32 * 1024 * 1024
        ),
    )(positions, normals, counts, screen))


def solution(mesh):
    placed = (
        P(None, None, "gx", "parts", None),
        P(None, None, "gx", "parts", None),
        P("gx", "parts", None),
        P("gx", "parts", None),
    )
    return jax.shard_map(
        functools.partial(local, mesh.shape["gx"]),
        mesh=mesh,
        in_specs=placed,
        out_specs=(P("gx", "parts", None), P("gx", "parts", None)),
        check_vma=False,
    )
```

time: 234 us -> 39.1 us (0.17)
  blocking collectives: 157 us -> 0 us
  Pallas kernels: 0 us -> 32.3 us
  other arithmetic: 31.6 us -> 0 us
  starting transfers between devices: 26.7 us -> 0 us
  waiting for transfers between devices: 8.26 us -> 0 us
  between operations: 7.92 us -> 0.65 us
  local copies, waits for them, and re-layouts: 1.45 us -> 5.93 us
    psum x5 -> x0, blocking collectives: 157 us -> none  [the longest x3 94.1 us: squares(): return lax.psum(jnp.sum(residual * residual), 'gx')]
    pallas_call x0 -> x1, Pallas kernels: none -> 32.3 us  [local(): pl.pallas_call(functools.partial(kernel, n, slots), out_shape=(out, out),...]
    ppermute x10 -> x0, starting transfers between devices: 26.7 us -> none  [the longest x5 20.3 us: with_halo(): before = lax.ppermute(last, axis, up)]
    add x32 -> x0, other arithmetic: 18 us -> none  [the longest x27 11.9 us: splat_cells(): accums[place] = accums[place] + vectors * (planar * along_z[third_off])]
    ppermute x10 -> x0, waiting for transfers between devices: 8.26 us -> none  [the longest x5 5.65 us: with_halo(): after = lax.ppermute(leading, axis, down)]
    mul x36 -> x0, other arithmetic: 5.35 us -> none  [splat_cells(): accums[place] = accums[place] + vectors * (planar * along_z[third_off])]
    unnamed x6 -> x10, local copies, waits for them, and re-layouts: 1.03 us -> 5.93 us
    reduce_sum x5 -> x0, other arithmetic: 4.83 us -> none  [the longest x3 3.56 us: local(): alpha = norm_now / lax.psum(jnp.sum(direction * image), 'gx')]
  transfers between devices with their start and end apart: 10 -> 0, of which waited for: 5 -> 0; matrix products, arithmetic and copies ran while one was open for 0% -> 0% of each run, Pallas kernels for 0% -> 0%
where the time goes in v1:
time: 39.1 us; the launch traced here: 38.9 us
  Pallas kernels  32.3 us (83%)
  local copies, waits for them, and re-layouts  5.93 us (15%)
  between operations  0.65 us (2%)
    pallas_call x1, Pallas kernels, local(): pl.pallas_call(functools.partial(kernel, n, slots), out_shape=(out, out),...  32.3 us
    unnamed x10, local copies, waits for them, and re-layouts  5.93 us

profile of v1, /device:TPU:0, one launch (start us, length us, event | category | flops | bytes accessed | tf_op | source)
XLA Modules:
  0.0 38.9 jit_solution(12430394117007749833)
XLA Ops:
  0.6 0.0 copy-start
  0.6 1.4 %copy-done = bf16[3,8,2,128,128]{4,3,2,1,0:T(8,128)(2,1)S(1)} copy-done((bf16[3,8,2,128,128]{4,3,2,1,0:T(8,128)(2,1)S(1)}, bf16[3,8,2,128,128]{4,3,2,1,0:T(8,128)(2,1)}, u32[]{:S(2)}) %copy-start) | copy-done | bytes 1572888
  2.0 0.0 copy-start.1
  2.0 1.4 %copy-done.1 = bf16[3,8,2,128,128]{4,3,2,1,0:T(8,128)(2,1)S(1)} copy-done((bf16[3,8,2,128,128]{4,3,2,1,0:T(8,128)(2,1)S(1)}, bf16[3,8,2,128,128]{4,3,2,1,0:T(8,128)(2,1)}, u32[]{:S(2)}) %copy-start.1) | copy-done | bytes 1572888
  3.4 0.0 copy-start.2
  3.5 0.9 %copy-done.2 = s32[2,128,128]{2,1,0:T(8,128)S(1)} copy-done((s32[2,128,128]{2,1,0:T(8,128)S(1)}, s32[2,128,128]{2,1,0:T(8,128)}, u32[]{:S(2)}) %copy-start.2) | copy-done | bytes 131096
  4.4 0.0 copy-start.3
  4.4 0.9 %copy-done.3 = f32[2,128,128]{2,1,0:T(8,128)S(1)} copy-done((f32[2,128,128]{2,1,0:T(8,128)S(1)}, f32[2,128,128]{2,1,0:T(8,128)}, u32[]{:S(2)}) %copy-start.3) | copy-done | bytes 131096
  5.3 32.3 %shard_map.59 = (f32[2,128,128]{2,1,0:T(8,128)S(1)}, f32[2,128,128]{2,1,0:T(8,128)S(1)}) custom-call(bf16[3,8,2,128,128]{4,3,2,1,0:T(8,128)(2,1)S(1)} %copy-done, bf16[3,8,2,128,128]{4,3,2,1,0:T(8,128)(2,1)S(1)} %copy-done.1, s32[2,128,128]{2,1,0:T(8,128)S(1)} %copy-done.2, f32[2,128,128]{2,1,0:T(8,128)S(1)} %copy-done.3), custom_call_target="tpu_custom_call" | custom-call | tf_op jit(solution)/shard_map/pallas_call | solution.py:301
  37.6 0.7 %copy.8 = f32[2,128,128]{2,1,0:T(8,128)} copy(f32[2,128,128]{2,1,0:T(8,128)S(1)} %get-tuple-element.4) | data formatting | bytes 262144
  38.2 0.7 %copy.9 = f32[2,128,128]{2,1,0:T(8,128)} copy(f32[2,128,128]{2,1,0:T(8,128)S(1)} %get-tuple-element.5) | data formatting | bytes 262144
Async XLA Ops:
  0.6 1.4 %copy-start = (bf16[3,8,2,128,128]{4,3,2,1,0:T(8,128)(2,1)S(1)}, bf16[3,8,2,128,128]{4,3,2,1,0:T(8,128)(2,1)}, u32[]{:S(2)}) copy-start(bf16[3,8,2,128,128]{4,3,2,1,0:T(8,128)(2,1)} %pos_hbm.1) | copy-start | bytes 4718596
  2.0 1.4 %copy-start.1 = (bf16[3,8,2,128,128]{4,3,2,1,0:T(8,128)(2,1)S(1)}, bf16[3,8,2,128,128]{4,3,2,1,0:T(8,128)(2,1)}, u32[]{:S(2)}) copy-start(bf16[3,8,2,128,128]{4,3,2,1,0:T(8,128)(2,1)} %nrm_hbm.1) | copy-start | bytes 4718596
  3.4 0.9 %copy-start.2 = (s32[2,128,128]{2,1,0:T(8,128)S(1)}, s32[2,128,128]{2,1,0:T(8,128)}, u32[]{:S(2)}) copy-start(s32[2,128,128]{2,1,0:T(8,128)} %cnt_hbm.1) | copy-start | bytes 393220
  4.4 0.9 %copy-start.3 = (f32[2,128,128]{2,1,0:T(8,128)S(1)}, f32[2,128,128]{2,1,0:T(8,128)}, u32[]{:S(2)}) copy-start(f32[2,128,128]{2,1,0:T(8,128)} %scr_hbm.1) | copy-start | bytes 393220

commit v2 on v1

--- a/solution.py
+++ b/solution.py
@@ -67,7 +67,7 @@
 
 
 def kernel(n, slots, pos_hbm, nrm_hbm, cnt_hbm, scr_hbm, sol_ref, res_ref,
-           pos, nrm, cnt, scr, g, out_l, out_r, in_l, in_r, v, halo, part, parts,
+           pos, nrm, cnt, scr, g, f0, out_l, out_r, in_l, in_r, v0, v1, v2, v3, part, parts,
            load_sem, send_sem, recv_sem, psend, precv):
     me = lax.axis_index("gx")
     my_part = lax.axis_index("parts")
@@ -89,7 +89,7 @@
     for k in range(chunks):
         for copy in loads(k):
             copy.start()
-    scr_copy = pltpu.make_async_copy(scr_hbm, scr, load_sem.at[3, 0])
+    scr_copy = pltpu.make_async_copy(scr_hbm, scr.at[2:4], load_sem.at[3, 0])
     scr_copy.start()
 
     barrier = pltpu.get_barrier_semaphore()
@@ -97,11 +97,64 @@
     @pl.loop(1, n)
     def _(d):
         pl.semaphore_signal(barrier, inc=1, device_id=peer(lax.rem(me + d, n)), device_id_type=MESH)
+
+    def ship(src, dst, by, at):
+        copy = pltpu.make_async_remote_copy(
+            src_ref=src, dst_ref=dst, send_sem=send_sem.at[at], recv_sem=recv_sem.at[at],
+            device_id=peer(jnp.clip(me + by, 0, n - 1)), device_id_type=MESH)
+        to, source = me + by, me - by
+        return copy, (to >= 0) & (to < n), (source >= 0) & (source < n)
+
+    ships = {
+        "screen": (ship(scr.at[2:4], scr.at[4:6], -1, 0), ship(scr.at[2:4], scr.at[0:2], 1, 1)),
+        "rim": (ship(out_l, in_r, -1, 2), ship(out_r, in_l, 1, 3)),
+        "first": (ship(v0.at[3], v0.at[5], -1, 4), ship(v0.at[4], v0.at[2], 1, 5)),
+        "second": (ship(v0.at[4], v0.at[6], -1, 6), ship(v0.at[3], v0.at[1], 1, 7)),
+        "third": (ship(v0.at[3], v0.at[7], -2, 8), ship(v0.at[4], v0.at[0], 2, 9)),
+    }
+
+    def begin(name):
+        for copy, sends, _ in ships[name]:
+            pl.when(sends)(copy.start)
+
+    def arrive(name):
+        for copy, _, receives in ships[name]:
+            pl.when(receives)(copy.wait_recv)
+
+    def sent(name):
+        for copy, sends, _ in ships[name]:
+            pl.when(sends)(copy.wait_send)
+
+    @pl.when(jnp.logical_not(has_left))
+    def _():
+        in_l[...] = jnp.zeros_like(in_l)
+        v0[1:3] = jnp.zeros_like(v0[1:3])
+        scr[0:2] = jnp.zeros_like(scr[0:2])
+
+    @pl.when(jnp.logical_not(has_right))
+    def _():
+        in_r[...] = jnp.zeros_like(in_r)
+        v0[5:7] = jnp.zeros_like(v0[5:7])
+        scr[4:6] = jnp.zeros_like(scr[4:6])
+
+    @pl.when(me < 2)
+    def _():
+        v0[0] = jnp.zeros_like(v0[0])
+
+    @pl.when(me >= n - 2)
+    def _():
+        v0[7] = jnp.zeros_like(v0[7])
 
     @pl.loop(0, chunks)
     def _(k):
         for copy in loads(k):
             copy.wait()
+
+        @pl.when(k == chunks - 1)
+        def _():
+            scr_copy.wait()
+            pl.semaphore_wait(barrier, n - 1)
+            begin("screen")
 
         @pl.loop(0, CHUNK // 16)
         def _(j):
@@ -139,90 +192,88 @@
 
     scale = 1.0 / 16.0
     for i in range(4):
-        v[i // 2, i % 2] = along_y(0, i)
-    out_l[0] = scale * v[0, 0]
-    out_l[1] = scale * (v[0, 1] + across(0))
-    out_r[0] = scale * (across(3) - v[1, 0])
-    out_r[1] = -scale * v[1, 1]
-
-    pl.semaphore_wait(barrier, n - 1)
-
-    def to_left(src, dst, at):
-        return pltpu.make_async_remote_copy(
-            src_ref=src, dst_ref=dst, send_sem=send_sem.at[0, at], recv_sem=recv_sem.at[0, at],
-            device_id=peer(jnp.maximum(me - 1, 0)), device_id_type=MESH)
-
-    def to_right(src, dst, at):
-        return pltpu.make_async_remote_copy(
-            src_ref=src, dst_ref=dst, send_sem=send_sem.at[1, at], recv_sem=recv_sem.at[1, at],
-            device_id=peer(jnp.minimum(me + 1, n - 1)), device_id_type=MESH)
-
-    pairs = [(to_left(out_l, in_r, 0), to_right(out_r, in_l, 0))]
-    for k in range(3):
-        pairs.append((to_left(v.at[k, 0], halo.at[k, 1], k + 1),
-                      to_right(v.at[k, 1], halo.at[k, 0], k + 1)))
-
-    def begin(at):
-        @pl.when(has_left)
-        def _():
-            pairs[at][0].start()
-
-        @pl.when(has_right)
-        def _():
-            pairs[at][1].start()
-
-    def arrive(at):
-        @pl.when(has_right)
-        def _():
-            pairs[at][0].wait_recv()
-
-        @pl.when(has_left)
-        def _():
-            pairs[at][1].wait_recv()
-
-    begin(0)
-    inner0 = across(1) + v[1, 0] - jnp.where(has_left, v[0, 0], 0.0)
-    inner1 = across(2) + jnp.where(has_right, v[1, 1], 0.0) - v[0, 1]
-    v[0, 0] = scale * inner0
-    v[0, 1] = scale * inner1
-    @pl.when(jnp.logical_not(has_left))
-    def _():
-        in_l[...] = jnp.zeros_like(in_l)
-        for k in range(3):
-            halo[k, 0] = jnp.zeros_like(halo[k, 0])
-
-    @pl.when(jnp.logical_not(has_right))
-    def _():
-        in_r[...] = jnp.zeros_like(in_r)
-        for k in range(3):
-            halo[k, 1] = jnp.zeros_like(halo[k, 1])
-
-    scr_copy.wait()
-    arrive(0)
-    v[0, 0] = v[0, 0] + (in_l[0] + in_r[0])
-    v[0, 1] = v[0, 1] + (in_l[1] + in_r[1])
-
-    def smooth(a, b, c):
-        u = a + (b + b) + c
-        u = row_before(u) + (u + u) + row_after(u)
-        return lane_before(u) + (u + u) + lane_after(u)
-
-    def fold(a):
-        return jnp.sum(a, axis=0, keepdims=True)
-
-    def dot(i, j):
-        return fold(v[i, 0] * v[j, 0] + v[i, 1] * v[j, 1])
-
-    for k in range(3):
-        begin(k + 1)
-        part[2 * k:2 * k + 1, :] = dot(k, k)
-        if k:
-            part[2 * k - 1:2 * k, :] = dot(k - 1, k)
-        arrive(k + 1)
-        a, b = v[k, 0], v[k, 1]
-        v[k + 1, 0] = (scr[0] + (4.0 - SHIFT)) * a - scale * smooth(halo[k, 0], a, b)
-        v[k + 1, 1] = (scr[1] + (4.0 - SHIFT)) * b - scale * smooth(a, b, halo[k, 1])
-    part[5:6, :] = dot(2, 3)
+        f0[i] = along_y(0, i)
+    out_l[0] = scale * f0[0]
+    out_l[1] = scale * (f0[1] + across(0))
+    out_r[0] = scale * (across(3) - f0[2])
+    out_r[1] = -scale * f0[3]
+    begin("rim")
+    inner0 = scale * (across(1) + f0[2] - jnp.where(has_left, f0[0], 0.0))
+    v0[3] = inner0
+    inner1 = scale * (across(2) + jnp.where(has_right, f0[3], 0.0) - f0[1])
+    v0[4] = inner1
+    arrive("rim")
+    v0[3] = v0[3] + (in_l[0] + in_r[0])
+    v0[4] = v0[4] + (in_l[1] + in_r[1])
+    for name in ("first", "second", "third"):
+        begin(name)
+
+    def smooth(a):
+        a = row_before(a) + (a + a) + row_after(a)
+        return lane_before(a) + (a + a) + lane_after(a)
+
+    def apply(src, dst, smoothed, i, lo):
+        u = smoothed[i] + (smoothed[i + 1] + smoothed[i + 1]) + smoothed[i + 2]
+        out = (scr[lo + i] + (4.0 - SHIFT)) * src[i + 1] - scale * u
+        if lo + i < 2:
+            out = jnp.where(has_left, out, 0.0)
+        if lo + i > 3:
+            out = jnp.where(has_right, out, 0.0)
+        dst[i] = out
+
+    def dot(a, i, b, j):
+        return jnp.sum(a[i] * b[j] + a[i + 1] * b[j + 1], axis=0, keepdims=True)
+
+    def smooth_into(dst, src, planes):
+        for i in planes:
+            dst[i] = smooth(src[i])
+
+    s0 = [g.at[0, i // 3, i % 3] for i in range(8)]
+    s1 = [g.at[1, i // 3, i % 3] for i in range(6)]
+    s2 = [g.at[2, i // 3, i % 3] for i in range(4)]
+
+    class Planes:
+        def __init__(self, refs):
+            self.refs = refs
+
+        def __getitem__(self, i):
+            return self.refs[i][...]
+
+        def __setitem__(self, i, value):
+            self.refs[i][...] = value
+
+    s0, s1, s2 = Planes(s0), Planes(s1), Planes(s2)
+    smooth_into(s0, v0, (3, 4))
+    part[0:1, :] = dot(v0, 3, v0, 3)
+    arrive("screen")
+    arrive("first")
+    smooth_into(s0, v0, (2, 5))
+    for i in (2, 3):
+        apply(v0, v1, s0, i, 0)
+    part[1:2, :] = dot(v0, 3, v1, 2)
+    part[2:3, :] = dot(v1, 2, v1, 2)
+    smooth_into(s1, v1, (2, 3))
+    arrive("second")
+    smooth_into(s0, v0, (1, 6))
+    for i in (1, 4):
+        apply(v0, v1, s0, i, 0)
+    smooth_into(s1, v1, (1, 4))
+    for i in (1, 2):
+        apply(v1, v2, s1, i, 1)
+    part[3:4, :] = dot(v1, 2, v2, 1)
+    part[4:5, :] = dot(v2, 1, v2, 1)
+    smooth_into(s2, v2, (1, 2))
+    arrive("third")
+    smooth_into(s0, v0, (0, 7))
+    for i in (0, 5):
+        apply(v0, v1, s0, i, 0)
+    smooth_into(s1, v1, (0, 5))
+    for i in (0, 3):
+        apply(v1, v2, s1, i, 1)
+    smooth_into(s2, v2, (0, 3))
+    for i in (0, 1):
+        apply(v2, v3, s2, i, 2)
+    part[5:6, :] = dot(v2, 1, v3, 0)
     part[6:8, :] = jnp.zeros((2, part.shape[1]), jnp.float32)
 
     def spread(d):
@@ -274,22 +325,15 @@
     sol = [s[0:1, :] for s in sol]
     res = [s[0:1, :] for s in res]
     for i in range(2):
-        sol_ref[i] = sol[0] * v[0, i] + sol[1] * v[1, i] + sol[2] * v[2, i]
-        res_ref[i] = res[0] * v[0, i] + res[1] * v[1, i] + res[2] * v[2, i] + res[3] * v[3, i]
+        sol_ref[i] = sol[0] * v0[3 + i] + sol[1] * v1[2 + i] + sol[2] * v2[1 + i]
+        res_ref[i] = res[0] * v0[3 + i] + res[1] * v1[2 + i] + res[2] * v2[1 + i] + res[3] * v3[i]
 
     @pl.loop(1, n)
     def _(d):
         spread(d).wait_send()
 
-    @pl.when(has_left)
-    def _():
-        for pair in pairs:
-            pair[0].wait_send()
-
-    @pl.when(has_right)
-    def _():
-        for pair in pairs:
-            pair[1].wait_send()
+    for name in ships:
+        sent(name)
 
 
 def local(n, positions, normals, counts, screen):
@@ -307,24 +351,27 @@
             pltpu.VMEM(positions.shape, positions.dtype),
             pltpu.VMEM(normals.shape, normals.dtype),
             pltpu.VMEM(counts.shape, counts.dtype),
-            pltpu.VMEM(screen.shape, f32),
+            pltpu.VMEM((6,) + plane, f32),
             pltpu.VMEM((3, 4, 3) + plane, f32),
-            pltpu.VMEM((2,) + plane, f32),
-            pltpu.VMEM((2,) + plane, f32),
-            pltpu.VMEM((2,) + plane, f32),
-            pltpu.VMEM((2,) + plane, f32),
-            pltpu.VMEM((4, 2) + plane, f32),
-            pltpu.VMEM((3, 2) + plane, f32),
+            pltpu.VMEM((4,) + plane, f32),
+            pltpu.VMEM((2,) + plane, f32),
+            pltpu.VMEM((2,) + plane, f32),
+            pltpu.VMEM((2,) + plane, f32),
+            pltpu.VMEM((2,) + plane, f32),
+            pltpu.VMEM((8,) + plane, f32),
+            pltpu.VMEM((6,) + plane, f32),
+            pltpu.VMEM((4,) + plane, f32),
+            pltpu.VMEM((2,) + plane, f32),
             pltpu.VMEM((8, 128), f32),
             pltpu.VMEM((n, 8, 128), f32),
             pltpu.SemaphoreType.DMA((4, chunks)),
-            pltpu.SemaphoreType.DMA((2, 4)),
-            pltpu.SemaphoreType.DMA((2, 4)),
+            pltpu.SemaphoreType.DMA((10,)),
+            pltpu.SemaphoreType.DMA((10,)),
             pltpu.SemaphoreType.DMA((n,)),
             pltpu.SemaphoreType.DMA((n,)),
         ],
         compiler_params=pltpu.CompilerParams(
-            collective_id=0, has_side_effects=True, vmem_limit_bytes=32 * 1024 * 1024
+            collective_id=0, has_side_effects=True, vmem_limit_bytes=60 * 1024 * 1024
         ),
     )(positions, normals, counts, screen))
 

time: 39.1 us -> 34.7 us (0.89)
  local copies, waits for them, and re-layouts: 5.93 us -> 3.14 us
  Pallas kernels: 32.3 us -> 30.8 us
    unnamed x10 -> x2, local copies, waits for them, and re-layouts: 5.93 us -> 3.14 us
    pallas_call x1, Pallas kernels: 32.3 us -> 30.8 us  [local(): pl.pallas_call(functools.partial(kernel, n, slots), out_shape=(out, out),...]
where the time goes in v2:
time: 34.7 us; the launch traced here: 34.6 us
  Pallas kernels  30.8 us (89%)
  local copies, waits for them, and re-layouts  3.14 us (9%)
  between operations  0.64 us (2%)
    pallas_call x1, Pallas kernels, local(): pl.pallas_call(functools.partial(kernel, n, slots), out_shape=(out, out),...  30.8 us
    unnamed x2, local copies, waits for them, and re-layouts  3.14 us

profile of v2, /device:TPU:0, one launch (start us, length us, event | category | flops | bytes accessed | tf_op | source)
XLA Modules:
  0.0 34.6 jit_solution(11282694981321475787)
XLA Ops:
  0.6 30.8 %shard_map.59 = (f32[2,128,128]{2,1,0:T(8,128)}, f32[2,128,128]{2,1,0:T(8,128)}) custom-call(bf16[3,8,2,128,128]{4,3,2,1,0:T(8,128)(2,1)} %pos_hbm.1, bf16[3,8,2,128,128]{4,3,2,1,0:T(8,128)(2,1)} %nrm_hbm.1, s32[2,128,128]{2,1,0:T(8,128)} %cnt_hbm.1, f32[2,128,128]{2,1,0:T(8,128)} %scr_hbm.1), custom_call_target="tpu_custom_call" | custom-call | tf_op jit(solution)/shard_map/pallas_call | solution.py:345
  31.4 1.6 %copy.8 = f32[2,128,128]{2,1,0:T(8,128)} copy(f32[2,128,128]{2,1,0:T(8,128)} %get-tuple-element.4) | data formatting | bytes 262144
  33.0 1.6 %copy.9 = f32[2,128,128]{2,1,0:T(8,128)} copy(f32[2,128,128]{2,1,0:T(8,128)} %get-tuple-element.5) | data formatting | bytes 262144

commit v3 on v2

--- a/solution.py
+++ b/solution.py
@@ -36,8 +36,8 @@
 
 
 def taps(m0, m1, m2):
-    twice = m1 + m1
-    return (m0 - twice) + m2, (m0 + twice) - (m2 + m2), m2
+    last = m1 - m2
+    return (m0 - m1) - m2, m0 + (m2 + m2), last
 
 
 def gather_moments(pos, nrm, cnt, c, rows, half, plane, slots):
@@ -52,15 +52,15 @@
         tx = jnp.where(live > s, n, 0.0)
         for p in range(3):
             if p:
-                tx = tx * x
+                tx = tx * (x if p == 1 else 1.0 - x)
             ty = tx
             for q in range(3):
                 if q:
-                    ty = ty * y
+                    ty = ty * (y if q == 1 else 1.0 - y)
                 tz = ty
                 for r in range(3):
                     if r:
-                        tz = tz * z
+                        tz = tz * (z if r == 1 else 1.0 - z)
                     at = 9 * p + 3 * q + r
                     sums[at] = tz if sums[at] is None else sums[at] + tz
     return sums
@@ -107,7 +107,8 @@
 
     ships = {
         "screen": (ship(scr.at[2:4], scr.at[4:6], -1, 0), ship(scr.at[2:4], scr.at[0:2], 1, 1)),
-        "rim": (ship(out_l, in_r, -1, 2), ship(out_r, in_l, 1, 3)),
+        "outer": (ship(out_l.at[0], in_r.at[0], -1, 2), ship(out_r.at[1], in_l.at[1], 1, 3)),
+        "inner": (ship(out_l.at[1], in_r.at[1], -1, 10), ship(out_r.at[0], in_l.at[0], 1, 11)),
         "first": (ship(v0.at[3], v0.at[5], -1, 4), ship(v0.at[4], v0.at[2], 1, 5)),
         "second": (ship(v0.at[4], v0.at[6], -1, 6), ship(v0.at[3], v0.at[1], 1, 7)),
         "third": (ship(v0.at[3], v0.at[7], -2, 8), ship(v0.at[4], v0.at[0], 2, 9)),
@@ -150,7 +151,7 @@
         for copy in loads(k):
             copy.wait()
 
-        @pl.when(k == chunks - 1)
+        @pl.when(k == chunks // 2)
         def _():
             scr_copy.wait()
             pl.semaphore_wait(barrier, n - 1)
@@ -161,8 +162,7 @@
             start = pl.multiple_of(k * CHUNK + j * 16, 16)
             rows = pl.ds(start, 16)
 
-            @pl.loop(0, 3)
-            def _(c):
+            for c in range(3):
                 for half in range(2):
                     low = gather_moments(pos, nrm, cnt, c, rows, half, 0, slots)
                     high = gather_moments(pos, nrm, cnt, c, rows, half, 1, slots)
@@ -191,18 +191,22 @@
         return (row_after(fy) - row_before(fy)) + (lane_after(fz) - lane_before(fz))
 
     scale = 1.0 / 16.0
-    for i in range(4):
-        f0[i] = along_y(0, i)
+    f0[0] = along_y(0, 0)
+    f0[3] = along_y(0, 3)
     out_l[0] = scale * f0[0]
+    out_r[1] = -scale * f0[3]
+    begin("outer")
+    f0[1] = along_y(0, 1)
+    f0[2] = along_y(0, 2)
     out_l[1] = scale * (f0[1] + across(0))
     out_r[0] = scale * (across(3) - f0[2])
-    out_r[1] = -scale * f0[3]
-    begin("rim")
+    begin("inner")
     inner0 = scale * (across(1) + f0[2] - jnp.where(has_left, f0[0], 0.0))
     v0[3] = inner0
     inner1 = scale * (across(2) + jnp.where(has_right, f0[3], 0.0) - f0[1])
     v0[4] = inner1
-    arrive("rim")
+    arrive("outer")
+    arrive("inner")
     v0[3] = v0[3] + (in_l[0] + in_r[0])
     v0[4] = v0[4] + (in_l[1] + in_r[1])
     for name in ("first", "second", "third"):
@@ -365,8 +369,8 @@
             pltpu.VMEM((8, 128), f32),
             pltpu.VMEM((n, 8, 128), f32),
             pltpu.SemaphoreType.DMA((4, chunks)),
-            pltpu.SemaphoreType.DMA((10,)),
-            pltpu.SemaphoreType.DMA((10,)),
+            pltpu.SemaphoreType.DMA((12,)),
+            pltpu.SemaphoreType.DMA((12,)),
             pltpu.SemaphoreType.DMA((n,)),
             pltpu.SemaphoreType.DMA((n,)),
         ],

time: 34.7 us -> 33 us (0.951)
  Pallas kernels: 30.8 us -> 29 us
    pallas_call x1, Pallas kernels: 30.8 us -> 29 us  [local(): pl.pallas_call(functools.partial(kernel, n, slots), out_shape=(out, out),...]
where the time goes in v3:
time: 33 us; the launch traced here: 32.8 us
  Pallas kernels  29 us (88%)
  local copies, waits for them, and re-layouts  3.14 us (10%)
  between operations  0.64 us (2%)
    pallas_call x1, Pallas kernels, local(): pl.pallas_call(functools.partial(kernel, n, slots), out_shape=(out, out),...  29 us
    unnamed x2, local copies, waits for them, and re-layouts  3.14 us

profile of v3, /device:TPU:0, one launch (start us, length us, event | category | flops | bytes accessed | tf_op | source)
XLA Modules:
  0.0 32.8 jit_solution(15705101774385160393)
XLA Ops:
  0.6 29.0 %shard_map.59 = (f32[2,128,128]{2,1,0:T(8,128)}, f32[2,128,128]{2,1,0:T(8,128)}) custom-call(bf16[3,8,2,128,128]{4,3,2,1,0:T(8,128)(2,1)} %pos_hbm.1, bf16[3,8,2,128,128]{4,3,2,1,0:T(8,128)(2,1)} %nrm_hbm.1, s32[2,128,128]{2,1,0:T(8,128)} %cnt_hbm.1, f32[2,128,128]{2,1,0:T(8,128)} %scr_hbm.1), custom_call_target="tpu_custom_call" | custom-call | tf_op jit(solution)/shard_map/pallas_call | solution.py:349
  29.7 1.6 %copy.8 = f32[2,128,128]{2,1,0:T(8,128)} copy(f32[2,128,128]{2,1,0:T(8,128)} %get-tuple-element.4) | data formatting | bytes 262144
  31.2 1.6 %copy.9 = f32[2,128,128]{2,1,0:T(8,128)} copy(f32[2,128,128]{2,1,0:T(8,128)} %get-tuple-element.5) | data formatting | bytes 262144

commit v4 on v3

--- a/solution.py
+++ b/solution.py
@@ -111,7 +111,8 @@
         "inner": (ship(out_l.at[1], in_r.at[1], -1, 10), ship(out_r.at[0], in_l.at[0], 1, 11)),
         "first": (ship(v0.at[3], v0.at[5], -1, 4), ship(v0.at[4], v0.at[2], 1, 5)),
         "second": (ship(v0.at[4], v0.at[6], -1, 6), ship(v0.at[3], v0.at[1], 1, 7)),
-        "third": (ship(v0.at[3], v0.at[7], -2, 8), ship(v0.at[4], v0.at[0], 2, 9)),
+        "third": (ship(v0.at[3], v0.at[7], -2, 8),),
+        "last": (ship(v0.at[4], v0.at[0], 2, 9),),
     }
 
     def begin(name):
@@ -268,16 +269,16 @@
     part[4:5, :] = dot(v2, 1, v2, 1)
     smooth_into(s2, v2, (1, 2))
     arrive("third")
-    smooth_into(s0, v0, (0, 7))
-    for i in (0, 5):
-        apply(v0, v1, s0, i, 0)
-    smooth_into(s1, v1, (0, 5))
-    for i in (0, 3):
-        apply(v1, v2, s1, i, 1)
-    smooth_into(s2, v2, (0, 3))
-    for i in (0, 1):
-        apply(v2, v3, s2, i, 2)
-    part[5:6, :] = dot(v2, 1, v3, 0)
+    smooth_into(s0, v0, (7,))
+    apply(v0, v1, s0, 5, 0)
+    smooth_into(s1, v1, (5,))
+    apply(v1, v2, s1, 3, 1)
+    smooth_into(s2, v2, (3,))
+    terms = [
+        v2[i] * ((scr[i + 1] + (4.0 - SHIFT)) * v2[i] - (2.0 * scale) * (s2[i] + s2[i + 1]))
+        for i in (1, 2)
+    ]
+    part[5:6, :] = jnp.sum(terms[0] + terms[1], axis=0, keepdims=True)
     part[6:8, :] = jnp.zeros((2, part.shape[1]), jnp.float32)
 
     def spread(d):
@@ -288,6 +289,16 @@
     @pl.loop(1, n)
     def _(d):
         spread(d).start()
+
+    begin("last")
+    arrive("last")
+    smooth_into(s0, v0, (0,))
+    apply(v0, v1, s0, 0, 0)
+    smooth_into(s1, v1, (0,))
+    apply(v1, v2, s1, 0, 1)
+    smooth_into(s2, v2, (0,))
+    for i in (0, 1):
+        apply(v2, v3, s2, i, 2)
 
     @pl.loop(1, n)
     def _(d):

time: 33 us -> 32.6 us (0.988)
    pallas_call x1, Pallas kernels: 29 us -> 28.7 us  [local(): pl.pallas_call(functools.partial(kernel, n, slots), out_shape=(out, out),...]
where the time goes in v4:
time: 32.6 us; the launch traced here: 32.5 us
  Pallas kernels  28.7 us (88%)
  local copies, waits for them, and re-layouts  3.14 us (10%)
  between operations  0.64 us (2%)
    pallas_call x1, Pallas kernels, local(): pl.pallas_call(functools.partial(kernel, n, slots), out_shape=(out, out),...  28.7 us
    unnamed x2, local copies, waits for them, and re-layouts  3.14 us

profile of v4, /device:TPU:0, one launch (start us, length us, event | category | flops | bytes accessed | tf_op | source)
XLA Modules:
  0.0 32.5 jit_solution(16383375449106223577)
XLA Ops:
  0.6 28.7 %shard_map.59 = (f32[2,128,128]{2,1,0:T(8,128)}, f32[2,128,128]{2,1,0:T(8,128)}) custom-call(bf16[3,8,2,128,128]{4,3,2,1,0:T(8,128)(2,1)} %pos_hbm.1, bf16[3,8,2,128,128]{4,3,2,1,0:T(8,128)(2,1)} %nrm_hbm.1, s32[2,128,128]{2,1,0:T(8,128)} %cnt_hbm.1, f32[2,128,128]{2,1,0:T(8,128)} %scr_hbm.1), custom_call_target="tpu_custom_call" | custom-call | tf_op jit(solution)/shard_map/pallas_call | solution.py:360
  29.3 1.6 %copy.8 = f32[2,128,128]{2,1,0:T(8,128)} copy(f32[2,128,128]{2,1,0:T(8,128)} %get-tuple-element.4) | data formatting | bytes 262144
  30.9 1.6 %copy.9 = f32[2,128,128]{2,1,0:T(8,128)} copy(f32[2,128,128]{2,1,0:T(8,128)} %get-tuple-element.5) | data formatting | bytes 262144
